TPU v7x, 32 devices: a whole 2x2x4 slice. The times are simulated.
32 devices in a mesh: parts: 2 (over y), ctx: 4 (over z), head: 4 (over x, core).
Axes of the slice: x: 2, y: 2, z: 4, core: 2. Of those that a mesh axis runs over, the one named last changes fastest.
Arguments:
- event_ids: int32 [8192], P(('parts', 'ctx')), parts along dimension 0, may hold values from 0 to 255
- embed_table: bfloat16 [256, 1024], replicated, may hold values from -6 to 6
- w_qkv: bfloat16 [1024, 3072], P(None, 'head'), may hold values from -0.1875 to 0.1875
- norm_gain: float32 [1024], P('head'), may hold values from 0.1 to 1.9
- w_out: bfloat16 [1024, 1024], P('head'), may hold values from -0.1875 to 0.1875
- init_state: float32 [8, 128, 128], P('head'), may hold values from -6 to 6
- out_grad: bfloat16 [8192, 1024], P(('parts', 'ctx')), parts along dimension 0, may hold values from -1 to 1
Outputs:
- layer_out: bfloat16 [8192, 1024], P(('parts', 'ctx'), 'head'), parts along dimension 0
- grad_wqkv: float32 [2048, 3072], P(('parts', 'ctx'), 'head'), parts along dimension 0
- grad_wout: float32 [2048, 1024], P(('parts', 'head'), 'ctx'), parts along dimension 0
- grad_gain: float32 [2048], P(('parts', 'head')), parts along dimension 0
- grad_init: float32 [16, 128, 128], P(('parts', 'head')), parts along dimension 0
- grad_table: float32 [512, 1024], P('parts'), parts along dimension 0
There are 2 independent parts, one for each index of `parts`. A program takes and returns all parts, laid end to end along the dimension named above; an argument that names none is the same for every part. Nothing has to cross between parts.
All inputs are finite; a program needn't handle non-finite values.
Results may differ from a plain program's by a relative error of at most 0.0082.
Values sent between devices are 32-bit elements; how exact they have to be, the bound alone decides.
A program may use at most 64 MiB of HBM per device.

v0:
```python
import jax
import jax.numpy as jnp
from jax import lax
from jax.sharding import PartitionSpec as P

BLOCK = 128
EPS = 1e-05


def prefix(part, axis, combine, identity, reverse):
    count = lax.axis_size(axis)
    place = lax.axis_index(axis)
    ahead = count - 1 - place if reverse else place
    gathered = lax.all_gather(part, axis)
    state = jnp.zeros_like(part) + jnp.asarray(identity, part.dtype)

    def one(step, state):
        source = count - 1 - step if reverse else step
        return combine(state, lax.dynamic_index_in_dim(gathered, source, 0, False))

    return lax.fori_loop(0, ahead, one, state)


def lower_mask(block_len):
    rows_idx = lax.broadcasted_iota(jnp.int32, (block_len, block_len), 0)
    cols_idx = lax.broadcasted_iota(jnp.int32, (block_len, block_len), 1)
    return rows_idx >= cols_idx


def add_states(earlier, later_one):
    return earlier + later_one


def contract_rows(left, right):
    return lax.dot_general(
        left, right, (((0,), (0,)), ((), ())), preferred_element_type=jnp.float32
    )


def contract_cols(left, right):
    return lax.dot_general(
        left, right, (((1,), (1,)), ((), ())), preferred_element_type=jnp.float32
    )


def per_device(event_ids, embed_table, w_qkv, norm_gain, w_out, init_state, out_grad):
    highest = lax.Precision.HIGHEST
    tok_rows = event_ids.shape[0]
    vocab_size = embed_table.shape[0]
    head_local = init_state.shape[0]
    head_dim = init_state.shape[1]
    block_len = BLOCK
    blocks = tok_rows // block_len
    one_hot = event_ids[:, None] == lax.broadcasted_iota(jnp.int32, (1, vocab_size), 1)
    embedded = jnp.dot(
        one_hot.astype(jnp.bfloat16), embed_table, preferred_element_type=jnp.float32
    ).astype(jnp.bfloat16)
    projected = jnp.dot(embedded, w_qkv, preferred_element_type=jnp.float32).astype(jnp.bfloat16)
    shaped = projected.reshape(blocks, block_len, head_local, 3, head_dim)
    queries = shaped[:, :, :, 0]
    key_rows = shaped[:, :, :, 1]
    value_rows = shaped[:, :, :, 2]
    block_kv = jnp.einsum(
        "bshd,bshe->bhde", key_rows, value_rows, preferred_element_type=jnp.float32
    )
    own_total = jnp.sum(block_kv, axis=0)
    zero_state = jnp.zeros_like(own_total)
    earlier_state = prefix(own_total, "ctx", add_states, zero_state, False)
    cumulative = jnp.cumsum(block_kv, axis=0)
    shifted = jnp.concatenate([jnp.zeros_like(block_kv[:1]), cumulative[:-1]], axis=0)
    states = init_state[None] + earlier_state[None] + shifted
    mask_tri = lower_mask(block_len)[None, None]
    scores = jnp.einsum("bthd,bshd->bhts", queries, key_rows, preferred_element_type=jnp.float32)
    scores_bf = jnp.where(mask_tri, scores, 0.0).astype(jnp.bfloat16)
    inter = jnp.einsum("bthd,bhde->bthe", queries.astype(jnp.float32), states, precision=highest)
    intra = jnp.einsum("bhts,bshe->bthe", scores_bf, value_rows, preferred_element_type=jnp.float32)
    raw_out = inter + intra
    inv_rms = lax.rsqrt(jnp.mean(raw_out * raw_out, axis=-1, keepdims=True) + EPS)
    normed = raw_out * inv_rms
    gain_view = norm_gain.reshape(head_local, head_dim)
    attn = (normed * gain_view).astype(jnp.bfloat16).reshape(tok_rows, head_local * head_dim)
    head_terms = jnp.dot(attn, w_out, preferred_element_type=jnp.float32)
    mixed = lax.psum_scatter(head_terms, "head", scatter_dimension=1, tiled=True)
    out_cols = mixed.shape[1]
    residual = lax.dynamic_slice_in_dim(embedded, lax.axis_index("head") * out_cols, out_cols, 1)
    layer_out = (residual.astype(jnp.float32) + mixed).astype(jnp.bfloat16)
    grad_attn = contract_cols(out_grad, w_out)
    grad_wout_local = contract_rows(attn, out_grad)
    normed_flat = normed.reshape(tok_rows, head_local * head_dim)
    grad_gain_local = jnp.sum(grad_attn * normed_flat, axis=0)
    grad_norm = (grad_attn * norm_gain).reshape(blocks, block_len, head_local, head_dim)
    grad_raw = inv_rms * (grad_norm - normed * jnp.mean(grad_norm * normed, axis=-1, keepdims=True))
    grad_bf = grad_raw.astype(jnp.bfloat16)
    grad_scores = jnp.einsum(
        "bthe,bshe->bhts", grad_bf, value_rows, preferred_element_type=jnp.float32
    )
    grad_scores = jnp.where(mask_tri, grad_scores, 0.0).astype(jnp.bfloat16)
    block_qg = jnp.einsum("bthd,bthe->bhde", queries, grad_bf, preferred_element_type=jnp.float32)
    own_grad = jnp.sum(block_qg, axis=0)
    later_state = prefix(own_grad, "ctx", add_states, zero_state, True)
    reversed_sum = jnp.cumsum(block_qg[::-1], axis=0)[::-1]
    local_after = jnp.concatenate([reversed_sum[1:], jnp.zeros_like(block_qg[:1])], axis=0)
    after = later_state[None] + local_after
    grad_q = jnp.einsum(
        "bthe,bhde->bthd", grad_bf.astype(jnp.float32), states, precision=highest
    ) + jnp.einsum("bhts,bshd->bthd", grad_scores, key_rows, preferred_element_type=jnp.float32)
    grad_k = jnp.einsum(
        "bshe,bhde->bshd", value_rows.astype(jnp.float32), after, precision=highest
    ) + jnp.einsum("bhts,bthd->bshd", grad_scores, queries, preferred_element_type=jnp.float32)
    grad_v = jnp.einsum(
        "bshd,bhde->bshe", key_rows.astype(jnp.float32), after, precision=highest
    ) + jnp.einsum("bhts,bthe->bshe", scores_bf, grad_bf, preferred_element_type=jnp.float32)
    grad_proj = (
        jnp.stack([grad_q, grad_k, grad_v], axis=3)
        .astype(jnp.bfloat16)
        .reshape(tok_rows, head_local * 3 * head_dim)
    )
    vocab_proj = contract_rows(one_hot.astype(jnp.bfloat16), grad_proj)
    vocab_cot = contract_rows(one_hot.astype(jnp.bfloat16), out_grad)
    summed_vocab, summed_wout, summed_gain, grad_init, summed_cot = lax.psum(
        (vocab_proj, grad_wout_local, grad_gain_local, own_grad, vocab_cot), "ctx"
    )
    summed_wqkv = lax.dot_general(
        embed_table.astype(jnp.float32),
        summed_vocab,
        (((0,), (0,)), ((), ())),
        precision=highest,
        preferred_element_type=jnp.float32,
    )
    head_table = lax.dot_general(
        summed_vocab,
        w_qkv.astype(jnp.float32),
        (((1,), (1,)), ((), ())),
        precision=highest,
        preferred_element_type=jnp.float32,
    )
    grad_table = lax.psum(head_table, "head") + summed_cot
    ctx_pos = lax.axis_index("ctx")
    width_rows = summed_wqkv.shape[0] // lax.axis_size("ctx")
    own_wqkv = lax.dynamic_slice_in_dim(summed_wqkv, ctx_pos * width_rows, width_rows, 0)
    own_wout = lax.dynamic_slice_in_dim(summed_wout, ctx_pos * width_rows, width_rows, 1)
    return (layer_out, own_wqkv, own_wout, summed_gain, grad_init, grad_table)


def solution(mesh):
    in_specs = (
        P(("parts", "ctx")),
        P(),
        P(None, "head"),
        P("head"),
        P("head", None),
        P("head", None, None),
        P(("parts", "ctx"), None),
    )
    out_specs = (
        P(("parts", "ctx"), "head"),
        P(("parts", "ctx"), "head"),
        P(("parts", "head"), "ctx"),
        P(("parts", "head")),
        P(("parts", "head"), None, None),
        P("parts", None),
    )
    return jax.shard_map(
        per_device, mesh=mesh, in_specs=in_specs, out_specs=out_specs, check_vma=False
    )
```

profile of v0, /device:TPU:0, one launch (start us, length us, event | category | flops | bytes accessed | tf_op | source)
XLA Modules:
  0.0 317.2 jit_solution(2077347792032638478)
XLA Ops:
  7.3 1.5 copy-done
  8.8 2.7 fusion.13
  11.4 0.8 convolution_convert_fusion
  12.2 1.3 copy-done.14
  13.6 3.0 convolution_convert_fusion.1
  16.5 2.6 copy.49
  19.1 1.8 copy.89
  21.0 1.1 fusion.47
  22.0 0.4 copy.88
  22.4 1.6 copy.87
  24.0 2.3 fusion.48
  26.3 18.0 %all-gather = f32[8,128,128]{2,1,0:T(8,128)} all-gather(f32[2,128,128]{2,1,0:T(8,128)S(1)} %get-tuple-element.134), channel_id=2, replica_groups=mesh['parts'=2,'ctx'=4,'head'=4] {'ctx'}, dimensions={0}, use_global_device_ids=true | all-gather | bytes 655360 | tf_op jit(solution)/shard_map/all_gather | solution.py:14
  44.4 1.4 fusion.50
  45.7 0.1 slice.26
  45.8 0.3 fusion.4
  46.1 0.5 copy-done.25
  46.6 1.0 fusion.16
  47.7 1.5 multiply_reduce_fusion.1
  49.2 2.1 broadcast_multiply_fusion
  51.3 2.7 reshape.58
  54.0 2.2 copy.59
  56.3 1.8 multiply_reduce_fusion
  58.1 1.1 multiply_convert_fusion
  59.2 0.6 copy-done.11
  59.8 1.6 fusion.15
  61.5 1.3 fusion.5
  62.8 1.5 fusion.49
  64.3 2.4 rev.4
  66.7 1.3 fusion.51
  68.0 1.0 slice.28
  69.0 2.2 slice.23
  71.2 19.9 %all-gather.1 = f32[8,128,128]{2,1,0:T(8,128)} all-gather(f32[2,128,128]{2,1,0:T(8,128)S(1)} %get-tuple-element.138), channel_id=3, replica_groups=mesh['parts'=2,'ctx'=4,'head'=4] {'ctx'}, dimensions={0}, use_global_device_ids=true | all-gather | bytes 655360 | tf_op jit(solution)/shard_map/all_gather | solution.py:14
  91.2 3.1 while.23
  91.2 0.9 bitcast_add_fusion.5
  92.1 0.9 bitcast_add_fusion.5
  93.1 0.9 bitcast_add_fusion.5
  94.3 2.5 fusion.18
  96.8 1.0 fusion.17
  97.8 0.3 copy.56
  98.2 1.7 fusion.20
  99.9 0.5 fusion.11
  100.4 0.5 copy-done.6
  100.9 0.4 fusion.10
  101.3 0.3 fusion.9
  101.6 0.2 pad_maximum_fusion
  101.8 1.0 copy.67
  102.8 1.7 fusion
  104.5 0.0 all-reduce.6.cloned.1.call-start
  104.6 116.2 %all-reduce.8.cloned.1.call-done = (f32[256,768]{1,0:T(8,128)}, f32[256,1024]{1,0:T(8,128)}, f32[2,128,128]{2,1,0:T(8,128)}, f32[256,1024]{1,0:T(8,128)}) async-done(((f32[256,768]{1,0:T(8,128)}, f32[256,1024]{1,0:T(8,128)}, f32[2,128,128]{2,1,0:T(8,128)}, f32[256,1024]{1,0:T(8,128)}), (f32[256,768]{1,0:T(8,128)}, f32[256,1024]{1,0:T(8,128)}, f32[2,128,128]{2,1,0:T(8,128)}, ...) | async-done | bytes 3014672 | tf_op jit(solution)/shard_map/psum | solution.py:120
  220.8 4.2 %fusion.53 = f32[256,1024]{1,0:T(8,128)} fusion(f32[256,768]{1,0:T(8,128)} %get-tuple-element.121, bf16[1024,768]{1,0:T(8,128)(2,1)} %param.13), kind=kOutput, calls=%fused_computation.80 | convolution fusion | flops 2415919104 | bytes 3407872 | tf_op jit(solution)/shard_map/dot_general | solution.py:130
  225.0 2.7 fusion.22
  227.8 1.2 copy-done.2
  229.0 1.3 copy.84
  230.3 1.8 fusion.12
  232.1 10.0 %psum.44 = f32[256]{0:T(256)} all-reduce(f32[256]{0:T(256)S(1)} %fusion.12), channel_id=1, replica_groups=mesh['parts'=2,'ctx'=4,'head'=4] {'ctx'}, use_global_device_ids=true, to_apply=%region_14.15 | all-reduce | flops 256 | bytes 2048 | tf_op jit(solution)/shard_map/psum | solution.py:120
  242.1 1.4 fusion.52
  243.5 0.1 dynamic-slice_bitcast_fusion
  243.6 1.1 copy.70
  244.8 1.7 constant_dynamic-slice_fusion
  246.4 13.7 %all-reduce.6.cloned.1.call-done = f32[256,1024]{1,0:T(8,128)} async-done(((f32[256,1024]{1,0:T(8,128)}), f32[256,1024]{1,0:T(8,128)}) %all-reduce.6.cloned.1.call-update) | async-done | bytes 1048592 | tf_op jit(solution)/shard_map/psum | solution.py:137
  260.1 2.7 add.133
  262.8 44.9 %reduce-scatter.2.cloned.1.call-done = f32[1024,256]{1,0:T(8,128)} async-done(((f32[1024,1024]{1,0:T(8,128)}), f32[1024,256]{1,0:T(8,128)}) %reduce-scatter.2.cloned.1.call-update) | async-done | bytes 1048592 | tf_op jit(solution)/shard_map/reduce_scatter | solution.py:83
  307.7 2.3 add_convert_fusion
  310.0 0.7 copy.130
  (64 shorter events, 0.3 us)
Async XLA Ops:
  7.2 1.6 copy-start
  7.2 4.2 %copy-start.28 = (s32[1024]{0:T(1024)S(1)}, s32[1024]{0:T(1024)}, u32[]{:S(2)}) copy-start(s32[1024]{0:T(1024)} %param.11) | copy-start | bytes 12292
  7.2 4.2 %copy-start.18 = (bf16[256,1024]{1,0:T(8,128)(2,1)S(1)}, bf16[256,1024]{1,0:T(8,128)(2,1)}, u32[]{:S(2)}) copy-start(bf16[256,1024]{1,0:T(8,128)(2,1)} %param.12) | copy-start | bytes 1572868
  7.2 213.6 %all-reduce.8.cloned.1.call-start = ((), (), s32[]{:S(2)}) async-start(), calls=%async_computation.3 | async-start | bytes 6029312 | tf_op jit(solution)/shard_map/psum | solution.py:120
  11.4 2.1 copy-start.23
  12.2 1.4 copy-start.14
  22.4 24.2 %copy-start.4 = (bf16[8,128,2,1,128]{4,1,2,0,3:T(8,128)(2,1)}, bf16[8,128,2,1,128]{4,1,2,0,3:T(8,128)(2,1)S(1)}, u32[]{:S(2)}) copy-start(bf16[8,128,2,1,128]{4,1,2,0,3:T(8,128)(2,1)S(1)} %copy.88) | copy-start | bytes 1572868
  44.3 1.5 copy-start.7
  45.7 0.9 copy-start.25
  45.8 1.9 copy-start.10
  46.1 3.1 copy-start.20
  47.7 1.5 copy-start.16
  47.7 1.5 copy-start.27
  56.3 1.9 copy-start.3
  58.1 3.4 %copy-start.1 = (f32[8,128,2,128]{1,3,2,0:T(8,128)}, f32[8,128,2,128]{1,3,2,0:T(8,128)S(1)}, u32[]{:S(2)}) copy-start(f32[8,128,2,128]{1,3,2,0:T(8,128)S(1)} %get-tuple-element.126) | copy-start | bytes 3145732
  58.1 1.8 copy-start.11
  59.8 3.0 copy-start.5
  64.3 6.9 %copy-start.24 = (f32[2,128,128]{2,1,0:T(8,128)}, f32[2,128,128]{2,1,0:T(8,128)S(1)}, u32[]{:S(2)}) copy-start(f32[2,128,128]{2,1,0:T(8,128)S(1)} %get-tuple-element.138) | copy-start | bytes 393220
  94.2 2.6 copy-start.8
  94.2 2.6 copy-start.9
  94.2 3.6 %copy-start.22 = (bf16[8,128,2,128]{1,3,2,0:T(8,128)(2,1)S(1)}, bf16[8,128,2,128]{1,3,2,0:T(8,128)(2,1)}, u32[]{:S(2)}) copy-start(bf16[8,128,2,128]{1,3,2,0:T(8,128)(2,1)} %get-tuple-element.131) | copy-start | bytes 1572868
  98.2 1.7 copy-start.12
  98.2 1.7 copy-start.13
  99.9 1.0 copy-start.6
  99.9 1.4 copy-start.21
  104.5 155.6 %all-reduce.6.cloned.1.call-start = ((), (), s32[]{:S(2)}) async-start(), calls=%async_computation.2 | async-start | bytes 2097152 | tf_op jit(solution)/shard_map/psum | solution.py:137
  220.8 4.2 %copy-start.17 = (bf16[256,1024]{1,0:T(8,128)(2,1)S(1)}, bf16[256,1024]{1,0:T(8,128)(2,1)}, u32[]{:S(2)}) copy-start(bf16[256,1024]{1,0:T(8,128)(2,1)} %param.15) | copy-start | bytes 1572868
  225.0 82.8 %reduce-scatter.2.cloned.1.call-start = ((), (), s32[]{:S(2)}) async-start(), calls=%async_computation.1 | async-start | bytes 5242880 | tf_op jit(solution)/shard_map/reduce_scatter | solution.py:83
  227.7 1.2 copy-start.2
  230.2 11.8 %copy-start.15 = (f32[256,768]{1,0:T(8,128)S(1)}, f32[256,768]{1,0:T(8,128)}, u32[]{:S(2)}) copy-start(f32[256,768]{1,0:T(8,128)} %get-tuple-element.121) | copy-start | bytes 2359300
  230.3 11.8 %copy-start.19 = (bf16[256,1024]{1,0:T(8,128)(2,1)S(1)}, bf16[256,1024]{1,0:T(8,128)(2,1)}, u32[]{:S(2)}) copy-start(bf16[256,1024]{1,0:T(8,128)(2,1)} %param.12) | copy-start | bytes 1572868
  260.1 49.9 %copy-start.26 = (f32[2,128,128]{2,1,0:T(8,128)S(1)}, f32[2,128,128]{2,1,0:T(8,128)}, u32[]{:S(2)}) copy-start(f32[2,128,128]{2,1,0:T(8,128)} %get-tuple-element.241) | copy-start | bytes 393220
Sparse Core Ops, SparseCore 0:
  104.6 116.0 all-reduce.7
  225.1 34.9 all-reduce.5
  262.8 44.8 reduce-scatter.1
where the time goes:
time: 318 us; the launch traced here: 317 us
  waiting for transfers between devices  175 us (55%)
  blocking collectives  47.9 us (15%)
  matrix products  34.4 us (11%)
  local copies, waits for them, and re-layouts  30.1 us (9%)
  other arithmetic  15.4 us (5%)
  between operations  14.2 us (4%)
    psum x1, waiting for transfers between devices, per_device(): lax.psum((vocab_proj, grad_wout_local, grad_gain_local, own_grad, vocab_c...  116 us
    reduce_scatter x1, waiting for transfers between devices, per_device(): lax.psum_scatter(head_terms, 'head', scatter_dimension=1, tiled=True)  44.9 us
    all_gather x2, blocking collectives, prefix(): gathered = lax.all_gather(part, axis)  37.9 us
    psum x1, waiting for transfers between devices, per_device(): grad_table = lax.psum(head_table, 'head') + summed_cot  13.7 us
    unnamed x63, local copies, waits for them, and re-layouts  11.4 us
    psum x1, blocking collectives, per_device(): lax.psum((vocab_proj, grad_wout_local, grad_gain_local, own_grad, vocab_c...  10 us
  transfers between devices with their start and end apart: 3, of which 3 were waited for; matrix products, arithmetic and copies ran while one was open for 4% of the time, Pallas kernels for 0%

commit v1 on v0

--- a/solution.py
+++ b/solution.py
@@ -44,6 +44,10 @@
 
 
 def per_device(event_ids, embed_table, w_qkv, norm_gain, w_out, init_state, out_grad):
+
+    def record_convert(mine_x):
+        return jnp.sum(lax.all_gather(mine_x, axis_name="head"), axis=0)
+
     highest = lax.Precision.HIGHEST
     tok_rows = event_ids.shape[0]
     vocab_size = embed_table.shape[0]
@@ -134,7 +138,7 @@
         precision=highest,
         preferred_element_type=jnp.float32,
     )
-    grad_table = lax.psum(head_table, "head") + summed_cot
+    grad_table = record_convert(head_table) + summed_cot
     ctx_pos = lax.axis_index("ctx")
     width_rows = summed_wqkv.shape[0] // lax.axis_size("ctx")
     own_wqkv = lax.dynamic_slice_in_dim(summed_wqkv, ctx_pos * width_rows, width_rows, 0)

time: 318 us -> 273 us (0.86)
  waiting for transfers between devices: 175 us -> 126 us
    reduce_scatter x1, waiting for transfers between devices: 44.9 us -> 0.01 us  [per_device(): lax.psum_scatter(head_terms, 'head', scatter_dimension=1, tiled=True)]
    psum x1 -> x0, waiting for transfers between devices: 13.7 us -> none  [per_device(): grad_table = lax.psum(head_table, 'head') + summed_cot]
    all_gather x0 -> x1, waiting for transfers between devices: none -> 13.6 us  [record_convert(): return jnp.sum(lax.all_gather(mine_x, axis_name='head'), axis=0)]
    psum x1, waiting for transfers between devices: 116 us -> 112 us  [per_device(): lax.psum((vocab_proj, grad_wout_local, grad_gain_local, own_grad, vocab_c...]
  transfers between devices with their start and end apart: 3 -> 3, of which waited for: 3 -> 2; matrix products, arithmetic and copies ran while one was open for 4% -> 6% of each run, Pallas kernels for 0% -> 0%
where the time goes in v1:
time: 273 us; the launch traced here: 272 us
  waiting for transfers between devices  126 us (46%)
  blocking collectives  47.9 us (18%)
  matrix products  34.4 us (13%)
  local copies, waits for them, and re-layouts  29.9 us (11%)
  other arithmetic  17.8 us (7%)
  between operations  15.9 us (6%)
    psum x1, waiting for transfers between devices, per_device(): lax.psum((vocab_proj, grad_wout_local, grad_gain_local, own_grad, vocab_c...  112 us
    all_gather x2, blocking collectives, prefix(): gathered = lax.all_gather(part, axis)  37.9 us
    all_gather x1, waiting for transfers between devices, record_convert(): return jnp.sum(lax.all_gather(mine_x, axis_name='head'), axis=0)  13.6 us
    unnamed x63, local copies, waits for them, and re-layouts  11.2 us
    psum x1, blocking collectives, per_device(): lax.psum((vocab_proj, grad_wout_local, grad_gain_local, own_grad, vocab_c...  10 us
    dot_general x3, matrix products, contract_rows(): lax.dot_general(left, right, (((0,), (0,)), ((), ())), preferred_element_...  6.04 us
  transfers between devices with their start and end apart: 3, of which 2 were waited for; matrix products, arithmetic and copies ran while one was open for 6% of the time, Pallas kernels for 0%

profile of v1, /device:TPU:0, one launch (start us, length us, event | category | flops | bytes accessed | tf_op | source)
XLA Modules:
  0.0 272.3 jit_solution(18029594449375735400)
XLA Ops:
  8.1 1.5 copy-done
  9.6 2.7 fusion.13
  12.3 0.8 convolution_convert_fusion
  13.0 1.4 copy-done.14
  14.4 3.0 %convolution_convert_fusion.1 = bf16[1024,768]{1,0:T(8,128)(2,1)} fusion(bf16[1024,1024]{1,0:T(8,128)(2,1)S(1)} %convolution_convert_fusion, bf16[1024,768]{1,0:T(8,128)(2,1)S(1)} %copy-done.23), kind=kOutput, calls=%fused_computation.3 | convolution fusion | flops 1611399168 | bytes 5242880 | tf_op jit(solution)/shard_map/dot_general | solution.py:62
  17.4 2.6 copy.49
  20.0 1.8 copy.89
  21.8 1.1 fusion.47
  22.9 0.4 copy.88
  23.3 1.6 copy.87
  24.9 2.3 fusion.48
  27.2 18.0 %all-gather = f32[8,128,128]{2,1,0:T(8,128)} all-gather(f32[2,128,128]{2,1,0:T(8,128)S(1)} %get-tuple-element.134), channel_id=2, replica_groups=mesh['parts'=2,'ctx'=4,'head'=4] {'ctx'}, dimensions={0}, use_global_device_ids=true | all-gather | bytes 655360 | tf_op jit(solution)/shard_map/all_gather | solution.py:14
  45.2 1.4 fusion.50
  46.6 0.1 slice.26
  46.7 0.3 fusion.4
  47.0 0.5 copy-done.25
  47.5 1.0 fusion.16
  48.5 1.5 multiply_reduce_fusion.1
  50.1 2.1 broadcast_multiply_fusion
  52.1 2.7 %reshape.59 = f32[8,128,2,128]{3,2,1,0:T(2,128)} reshape(f32[1024,256]{1,0:T(8,128)} %get-tuple-element.132) | data formatting | bytes 2097152 | tf_op jit(solution)/shard_map/reshape | solution.py:95
  54.9 2.2 copy.59
  57.1 1.8 multiply_reduce_fusion
  59.0 1.1 multiply_convert_fusion
  60.1 0.6 copy-done.11
  60.7 1.6 fusion.15
  62.3 1.3 fusion.5
  63.7 1.5 fusion.49
  65.2 2.4 rev.4
  67.5 1.3 fusion.51
  68.8 1.0 slice.28
  69.8 2.2 slice.23
  72.1 19.9 %all-gather.1 = f32[8,128,128]{2,1,0:T(8,128)} all-gather(f32[2,128,128]{2,1,0:T(8,128)S(1)} %get-tuple-element.138), channel_id=3, replica_groups=mesh['parts'=2,'ctx'=4,'head'=4] {'ctx'}, dimensions={0}, use_global_device_ids=true | all-gather | bytes 655360 | tf_op jit(solution)/shard_map/all_gather | solution.py:14
  92.0 3.1 %while.23 = (s32[]{:T(128)}, f32[2,128,128]{2,1,0:T(8,128)S(1)}, s32[]{:T(128)}, f32[4,2,128,128]{3,2,1,0:T(8,128)}, s32[]{:T(128)}, /*index=5*/s32[]{:T(128)}, s32[]{:T(128)}, s32[]{:T(128)}) while((s32[]{:T(128)}, f32[2,128,128]{2,1,0:T(8,128)S(1)}, s32[]{:T(128)}, f32[4,2,128,128]{3,2,1,0:T(8,128)}, s32[]{:T(128)}, /*index=5*/s32[]{:T(128)}, ...), condition=%wide.region_9.10_spmd, body=%wide.region_8.9_spmd.sunk | while | flops 32774 | bytes 393359 | solution.py:21
  92.0 0.9 bitcast_add_fusion.5
  93.0 0.9 bitcast_add_fusion.5
  93.9 0.9 bitcast_add_fusion.5
  95.1 2.5 fusion.18
  97.6 1.0 fusion.17
  98.7 0.3 copy.56
  99.0 1.7 fusion.20
  100.7 0.5 fusion.11
  101.2 0.5 copy-done.6
  101.8 0.4 fusion.10
  102.1 0.3 fusion.9
  102.4 0.2 pad_maximum_fusion
  102.6 1.0 copy.67
  103.6 1.7 fusion
  105.4 1.0 copy-done.17
  106.4 2.7 %fusion.22 = f32[1024,1024]{1,0:T(8,128)} fusion(bf16[256,1024]{1,0:T(8,128)(2,1)S(1)} %copy-done.17, bf16[32,8,8,128]{3,2,1,0:T(8,128)(2,1)S(1)} %bitcast.110), kind=kOutput, calls=%fused_computation.42 | convolution fusion | flops 536870912 | bytes 5242880 | tf_op jit(solution)/shard_map/dot_general | solution.py:86
  109.1 0.0 all-gather.5.cloned.1.call-start
  109.2 112.4 %all-reduce.5.cloned.1.call-done = (f32[256,768]{1,0:T(8,128)}, f32[256,1024]{1,0:T(8,128)}, f32[2,128,128]{2,1,0:T(8,128)}, f32[256,1024]{1,0:T(8,128)}) async-done(((f32[256,768]{1,0:T(8,128)}, f32[256,1024]{1,0:T(8,128)}, f32[2,128,128]{2,1,0:T(8,128)}, f32[256,1024]{1,0:T(8,128)}), (f32[256,768]{1,0:T(8,128)}, f32[256,1024]{1,0:T(8,128)}, f32[2,128,128]{2,1,0:T(8,128)}, ...) | async-done | bytes 3014672 | tf_op jit(solution)/shard_map/psum | solution.py:124
  221.6 4.2 %fusion.53 = f32[256,1024]{1,0:T(8,128)} fusion(f32[256,768]{1,0:T(8,128)} %get-tuple-element.121, bf16[1024,768]{1,0:T(8,128)(2,1)} %param.13), kind=kOutput, calls=%fused_computation.80 | convolution fusion | flops 2415919104 | bytes 3407872 | tf_op jit(solution)/shard_map/dot_general | solution.py:134
  225.8 1.3 copy.84
  227.1 1.8 fusion.12
  228.9 10.0 %psum.37 = f32[256]{0:T(256)} all-reduce(f32[256]{0:T(256)S(1)} %fusion.12), channel_id=1, replica_groups=mesh['parts'=2,'ctx'=4,'head'=4] {'ctx'}, use_global_device_ids=true, to_apply=%region_14.15 | all-reduce | flops 256 | bytes 2048 | tf_op jit(solution)/shard_map/psum | solution.py:124
  238.9 1.4 fusion.52
  240.4 0.1 dynamic-slice_bitcast_fusion
  240.5 1.1 copy.70
  241.6 1.7 constant_dynamic-slice_fusion
  243.3 2.3 add_convert_fusion
  245.5 13.6 %all-gather.5.cloned.1.call-done = f32[1024,1024]{1,0:T(8,128)} async-done(((f32[256,1024]{1,0:T(8,128)}), f32[1024,1024]{1,0:T(8,128)}) %all-gather.5.cloned.1.call-update) | async-done | bytes 4194320 | tf_op jit(solution)/shard_map/all_gather | solution.py:49
  259.1 2.7 reduce_sum.59
  261.8 2.4 add.131
  264.2 0.7 copy.130
  (65 shorter events, 0.4 us)
Async XLA Ops:
  8.0 1.6 copy-start
  8.0 4.2 %copy-start.28 = (s32[1024]{0:T(1024)S(1)}, s32[1024]{0:T(1024)}, u32[]{:S(2)}) copy-start(s32[1024]{0:T(1024)} %param.11) | copy-start | bytes 12292
  8.0 4.2 %copy-start.18 = (bf16[256,1024]{1,0:T(8,128)(2,1)S(1)}, bf16[256,1024]{1,0:T(8,128)(2,1)}, u32[]{:S(2)}) copy-start(bf16[256,1024]{1,0:T(8,128)(2,1)} %param.12) | copy-start | bytes 1572868
  8.0 213.6 %all-reduce.5.cloned.1.call-start = ((), (), s32[]{:S(2)}) async-start(), calls=%async_computation.3 | async-start | bytes 6029312 | tf_op jit(solution)/shard_map/psum | solution.py:124
  12.3 2.1 copy-start.23
  13.0 1.4 copy-start.14
  23.3 24.2 %copy-start.4 = (bf16[8,128,2,1,128]{4,1,2,0,3:T(8,128)(2,1)}, bf16[8,128,2,1,128]{4,1,2,0,3:T(8,128)(2,1)S(1)}, u32[]{:S(2)}) copy-start(bf16[8,128,2,1,128]{4,1,2,0,3:T(8,128)(2,1)S(1)} %copy.88) | copy-start | bytes 1572868
  45.2 1.5 copy-start.7
  46.6 0.9 copy-start.25
  46.7 1.9 copy-start.10
  47.0 3.1 %copy-start.20 = (bf16[8,2,128,128]{3,2,1,0:T(8,128)(2,1)}, bf16[8,2,128,128]{3,2,1,0:T(8,128)(2,1)S(1)}, u32[]{:S(2)}) copy-start(bf16[8,2,128,128]{3,2,1,0:T(8,128)(2,1)S(1)} %fusion.4) | copy-start | bytes 1572868
  48.5 1.5 copy-start.16
  48.5 1.5 copy-start.27
  57.1 1.9 copy-start.3
  58.9 3.4 %copy-start.1 = (f32[8,128,2,128]{1,3,2,0:T(8,128)}, f32[8,128,2,128]{1,3,2,0:T(8,128)S(1)}, u32[]{:S(2)}) copy-start(f32[8,128,2,128]{1,3,2,0:T(8,128)S(1)} %get-tuple-element.126) | copy-start | bytes 3145732
  58.9 1.8 copy-start.11
  60.7 3.0 %copy-start.5 = (bf16[8,128,2,1,128]{4,1,2,0,3:T(8,128)(2,1)S(1)}, bf16[8,128,2,1,128]{4,1,2,0,3:T(8,128)(2,1)}, u32[]{:S(2)}) copy-start(bf16[8,128,2,1,128]{4,1,2,0,3:T(8,128)(2,1)} %copy-done.4) | copy-start | bytes 1572868
  65.2 6.9 %copy-start.24 = (f32[2,128,128]{2,1,0:T(8,128)}, f32[2,128,128]{2,1,0:T(8,128)S(1)}, u32[]{:S(2)}) copy-start(f32[2,128,128]{2,1,0:T(8,128)S(1)} %get-tuple-element.138) | copy-start | bytes 393220
  95.1 2.6 copy-start.8
  95.1 2.6 copy-start.9
  95.1 3.6 %copy-start.22 = (bf16[8,128,2,128]{1,3,2,0:T(8,128)(2,1)S(1)}, bf16[8,128,2,128]{1,3,2,0:T(8,128)(2,1)}, u32[]{:S(2)}) copy-start(bf16[8,128,2,128]{1,3,2,0:T(8,128)(2,1)} %get-tuple-element.131) | copy-start | bytes 1572868
  99.0 1.7 copy-start.12
  99.0 1.7 copy-start.13
  100.7 1.0 copy-start.6
  100.7 1.4 copy-start.21
  105.3 1.0 copy-start.17
  105.4 137.9 %reduce-scatter.2.cloned.1.call-start = ((), (), s32[]{:S(2)}) async-start(), calls=%async_computation.1 | async-start | bytes 5242880 | tf_op jit(solution)/shard_map/reduce_scatter | solution.py:87
  109.1 150.0 %all-gather.5.cloned.1.call-start = ((), (), s32[]{:S(2)}) async-start(), calls=%async_computation.2 | async-start | bytes 5242880 | tf_op jit(solution)/shard_map/all_gather | solution.py:49
  221.6 4.2 %copy-start.2 = (f32[8,128,2,128]{1,3,2,0:T(8,128)S(1)}, f32[8,128,2,128]{1,3,2,0:T(8,128)}, u32[]{:S(2)}) copy-start(f32[8,128,2,128]{1,3,2,0:T(8,128)} %copy-done.1) | copy-start | bytes 3145732
  227.1 11.8 %copy-start.15 = (f32[256,768]{1,0:T(8,128)S(1)}, f32[256,768]{1,0:T(8,128)}, u32[]{:S(2)}) copy-start(f32[256,768]{1,0:T(8,128)} %get-tuple-element.121) | copy-start | bytes 2359300
  227.1 11.8 %copy-start.19 = (bf16[256,1024]{1,0:T(8,128)(2,1)S(1)}, bf16[256,1024]{1,0:T(8,128)(2,1)}, u32[]{:S(2)}) copy-start(bf16[256,1024]{1,0:T(8,128)(2,1)} %param.12) | copy-start | bytes 1572868
  261.8 2.4 copy-start.26
Sparse Core Ops, SparseCore 0:
  105.5 116.0 all-reduce.4
Sparse Core Ops, SparseCore 1:
  109.2 42.6 reduce-scatter.1
  225.9 33.2 all-gather.4
